TPU v7x, 128 devices: a whole 4x4x4 slice. The times are simulated.
128 devices in a mesh: user: 16 (over z, y_lo, core), item: 8 (over x, y_hi).
Axes of the slice: x: 4, y: 4 (y_hi: 2, y_lo: 2; y = y_hi * 2 + y_lo), z: 4, core: 2. Of those that a mesh axis runs over, the one named last changes fastest.
Arguments:
- user_table: float32 [16384, 256], P(('user', 'item')), may hold values from -1.5 to 1.5
- user_state: float32 [16384], P(('user', 'item')), may hold values from 0.001 to 0.1
- item_table: float32 [32768, 256], P(('item', 'user')), may hold values from -1.5 to 1.5
- item_state: float32 [32768], P(('item', 'user')), may hold values from 0.001 to 0.1
- edge_users: int32 [16, 8, 2048], P('user', 'item'), may hold values from 0 to 1023
- edge_items: int32 [16, 8, 2048], P('user', 'item'), may hold values from 0 to 4095
- negatives: int32 [8, 1024], P('item'), may hold values from 0 to 4095
Outputs:
- new_user_table: float32 [16384, 256], P(('user', 'item'))
- new_user_state: float32 [16384], P(('user', 'item'))
- new_item_table: float32 [32768, 256], P(('item', 'user'))
- new_item_state: float32 [32768], P(('item', 'user'))
All inputs are finite; a program needn't handle non-finite values.
Results may differ from a plain program's by a relative error of at most 0.0017.
Values may be sent and summed in bfloat16 or wider, within the bound.
A program may use at most 64 MiB of HBM per device.

v0:
```python
import jax
import jax.numpy as jnp
from jax import lax
from jax.sharding import PartitionSpec as P

learn_rate = 0.1


def adagrad(table, state, gradient):
    new_state = state + jnp.mean(gradient * gradient, axis=1)
    return (table - learn_rate * gradient / jnp.sqrt(new_state)[:, None], new_state)


def take_rows(wanted, shard_rows):
    span = shard_rows.shape[0]
    one_hot = (wanted[:, None] == lax.iota(jnp.int32, span)[None, :]).astype(jnp.bfloat16)
    return jnp.dot(one_hot, shard_rows, preferred_element_type=jnp.float32)


def spread_rows(wanted, values, row_count):
    one_hot = (lax.iota(jnp.int32, row_count)[:, None] == wanted[None, :]).astype(jnp.bfloat16)
    return jnp.dot(one_hot, values, preferred_element_type=jnp.float32)


def per_device(user_table, user_state, item_table, item_state, edge_users, edge_items, negatives):
    user_index = edge_users.reshape(-1)
    item_index = edge_items.reshape(-1)
    negative_index = negatives.reshape(-1)
    negative_count = negative_index.shape[0]
    user_owned = user_table.shape[0]
    item_owned = item_table.shape[0]
    picked_users = take_rows(
        user_index, lax.all_gather(user_table.astype(jnp.bfloat16), "item", axis=0, tiled=True)
    ).astype(jnp.bfloat16)
    shard_rows = lax.all_gather(item_table.astype(jnp.bfloat16), "user", axis=0, tiled=True)
    items_float = take_rows(item_index, shard_rows)
    negatives_float = take_rows(negative_index, shard_rows)
    picked_items = items_float.astype(jnp.bfloat16)
    picked_negatives = negatives_float.astype(jnp.bfloat16)
    positive = jnp.sum(picked_users.astype(jnp.float32) * picked_items.astype(jnp.float32), axis=1)
    negative_scores = jnp.dot(picked_users, picked_negatives.T, preferred_element_type=jnp.float32)
    weights = (jax.nn.sigmoid(negative_scores) / negative_count).astype(jnp.bfloat16)
    pull = jax.nn.sigmoid(-positive)[:, None]
    user_grad = (
        -pull * picked_items.astype(jnp.float32)
        + jnp.dot(weights, picked_negatives, preferred_element_type=jnp.float32)
    ).astype(jnp.bfloat16)
    item_grad = (-pull * picked_users.astype(jnp.float32)).astype(jnp.bfloat16)
    negative_grad = jnp.dot(weights.T, picked_users, preferred_element_type=jnp.float32).astype(
        jnp.bfloat16
    )
    user_total = lax.psum_scatter(
        spread_rows(user_index, user_grad, user_owned * lax.axis_size("item")),
        "item",
        scatter_dimension=0,
        tiled=True,
    )
    item_total = lax.psum_scatter(
        spread_rows(item_index, item_grad, item_owned * lax.axis_size("user"))
        + spread_rows(negative_index, negative_grad, item_owned * lax.axis_size("user")),
        "user",
        scatter_dimension=0,
        tiled=True,
    )
    new_user_table, new_user_state = adagrad(user_table, user_state, user_total)
    new_item_table, new_item_state = adagrad(item_table, item_state, item_total)
    return (new_user_table, new_user_state, new_item_table, new_item_state)


def solution(mesh):
    in_specs = (
        P(("user", "item"), None),
        P(("user", "item")),
        P(("item", "user"), None),
        P(("item", "user")),
        P("user", "item", None),
        P("user", "item", None),
        P("item", None),
    )
    out_specs = (
        P(("user", "item"), None),
        P(("user", "item")),
        P(("item", "user"), None),
        P(("item", "user")),
    )
    return jax.shard_map(
        per_device, mesh=mesh, in_specs=in_specs, out_specs=out_specs, check_vma=False
    )
```

profile of v0, /device:TPU:1, one launch (start us, length us, event | category | flops | bytes accessed | tf_op | source)
XLA Modules:
  0.0 225.4 jit_solution(11815348404063712578)
XLA Ops:
  7.2 0.0 all-gather.2.cloned.1.call-start
  7.2 1.6 convert_element_type.44
  8.8 0.0 all-gather.2.cloned.1.call-update
  8.9 0.0 reduce-scatter.3.cloned.1.call-start
  8.9 0.9 convert_element_type.41
  9.8 0.0 copy-start.6
  9.8 30.4 %all_gather.6 = bf16[1024,256]{1,0:T(8,128)(2,1)S(1)} all-gather(bf16[128,256]{1,0:T(8,128)(2,1)S(1)} %convert_element_type.41), channel_id=1, replica_groups=mesh['user'=16,'item'=8] {'item'}, dimensions={0}, use_global_device_ids=true | all-gather | bytes 589824 | tf_op jit(solution)/shard_map/all_gather | solution.py:33
  40.2 3.0 %fusion.13 = bf16[2048,256]{0,1:T(8,128)(2,1)S(1)} fusion(bf16[1024,256]{1,0:T(8,128)(2,1)S(1)} %all_gather.6, s32[2048]{0:T(1024)} %bitcast.13), kind=kOutput, calls=%fused_computation.24 | convolution fusion | flops 1076363264 | bytes 1581056 | tf_op jit(solution)/shard_map/dot_general | solution.py:17
  43.2 6.0 %all-gather.2.cloned.1.call-done = bf16[4096,256]{1,0:T(8,128)(2,1)} async-done(((bf16[256,256]{1,0:T(8,128)(2,1)}), bf16[4096,256]{1,0:T(8,128)(2,1)}) %all-gather.2.cloned.1.call-update) | async-done | bytes 2097168 | tf_op jit(solution)/shard_map/all_gather | solution.py:35
  49.2 0.0 copy-done.6
  49.2 0.0 copy-start.4
  49.2 0.0 copy-start.7
  49.2 9.4 %fusion.17 = (f32[2048]{0:T(1024)S(1)}, bf16[2048,256]{0,1:T(8,128)(2,1)S(1)}) fusion(bf16[2048,256]{0,1:T(8,128)(2,1)S(1)} %fusion.13, bf16[4096,256]{1,0:T(8,128)(2,1)} %all-gather.2.cloned.1.call-done, s32[2048]{0:T(1024)S(1)} %bitcast.15), kind=kOutput, calls=%fused_computation.28 | convolution fusion | flops 4305975296 | bytes 4210688 | tf_op jit(solution)/shard_map/dot_general | solution.py:17
  58.7 0.0 copy-done.4
  58.7 0.0 copy-done.7
  58.7 2.9 %fusion.18 = bf16[1024,256]{1,0:T(8,128)(2,1)S(1)} fusion(bf16[4096,256]{1,0:T(8,128)(2,1)S(1)} %copy-done.4, s32[1024]{0:T(1024)S(1)} %bitcast.17), kind=kOutput, calls=%fused_computation.29 | convolution fusion | flops 2151940096 | bytes 2625536 | tf_op jit(solution)/shard_map/dot_general | solution.py:17
  61.6 0.0 copy-start.5
  61.6 4.5 %multiply_convert_fusion = bf16[2048,1024]{1,0:T(8,128)(2,1)} fusion(bf16[2048,256]{0,1:T(8,128)(2,1)S(1)} %fusion.13, bf16[1024,256]{1,0:T(8,128)(2,1)S(1)} %fusion.18), kind=kOutput, calls=%fused_computation.11 | convolution fusion | flops 1084227584 | bytes 5767168 | tf_op jit(solution)/shard_map/dot_general | solution.py:41
  66.1 0.0 copy-done.5
  66.1 6.0 %fusion.8 = f32[1024,256]{1,0:T(8,128)} fusion(s32[2048]{0:T(1024)S(1)} %bitcast.14, bf16[2048,1024]{1,0:T(8,128)(2,1)} %multiply_convert_fusion, bf16[1024,256]{1,0:T(8,128)(2,1)S(1)} %fusion.18, bf16[2048,256]{0,1:T(8,128)(2,1)S(1)} %get-tuple-element.9, f32[2048]{0:T(1024)S(1)} %divide_negate_fusion), kind=kOutput, calls=%fused_computation.15 | convolution fusion | flops 2151677952 | bytes 6832128 | tf_op jit(solution)/shard_map/dot_general | solution.py:22
  72.1 0.0 reduce-scatter.3.cloned.1.call-update
  72.1 0.0 reduce-scatter.5.cloned.1.call-start
  72.2 3.5 %convolution_convert_fusion = bf16[1024,256]{1,0:T(8,128)(2,1)S(1)} fusion(bf16[2048,1024]{1,0:T(8,128)(2,1)} %multiply_convert_fusion, bf16[2048,256]{0,1:T(8,128)(2,1)S(1)} %fusion.13), kind=kOutput, calls=%fused_computation.30 | convolution fusion | flops 1074003968 | bytes 5767168 | tf_op jit(solution)/shard_map/dot_general | solution.py:49
  75.7 3.1 %fusion.5 = f32[4096,256]{1,0:T(8,128)S(1)} fusion(bf16[1024,256]{1,0:T(8,128)(2,1)S(1)} %convolution_convert_fusion, s32[1024]{0:T(1024)S(1)} %bitcast.18), kind=kOutput, calls=%fused_computation.9 | convolution fusion | flops 2151677952 | bytes 4722688 | tf_op jit(solution)/shard_map/dot_general | solution.py:22
  78.9 8.2 %fusion.10 = f32[4096,256]{1,0:T(8,128)} fusion(f32[4096,256]{1,0:T(8,128)S(1)} %fusion.5, s32[2048]{0:T(1024)S(1)} %bitcast.16, bf16[2048,256]{0,1:T(8,128)(2,1)S(1)} %fusion.13, f32[2048]{0:T(1024)S(1)} %divide_negate_fusion), kind=kOutput, calls=%fused_computation.17 | convolution fusion | flops 4305977344 | bytes 9453568 | tf_op jit(solution)/shard_map/dot_general | solution.py:22
  87.0 0.0 copy-start.3
  87.0 0.0 copy-start.1
  87.0 0.0 copy-start.2
  87.0 0.0 copy-start
  87.0 0.0 reduce-scatter.5.cloned.1.call-update
  87.0 57.2 %reduce-scatter.3.cloned.1.call-done = f32[128,256]{1,0:T(8,128)} async-done(((f32[1024,256]{1,0:T(8,128)}), f32[128,256]{1,0:T(8,128)}) %reduce-scatter.3.cloned.1.call-update) | async-done | bytes 131088 | tf_op jit(solution)/shard_map/reduce_scatter | solution.py:52
  144.2 1.0 multiply_reduce_fusion.1
  145.2 0.0 copy-done.3
  145.2 0.5 fusion.22
  145.7 0.0 copy-done.1
  145.7 1.7 divide_subtract_fusion.1
  147.4 68.1 %reduce-scatter.5.cloned.1.call-done = f32[256,256]{1,0:T(8,128)} async-done(((f32[4096,256]{1,0:T(8,128)}), f32[256,256]{1,0:T(8,128)}) %reduce-scatter.5.cloned.1.call-update) | async-done | bytes 262160 | tf_op jit(solution)/shard_map/reduce_scatter | solution.py:58
  215.5 1.1 multiply_reduce_fusion
  216.5 0.0 copy-done.2
  216.5 0.6 fusion.21
  217.1 0.0 copy-done
  217.1 1.8 divide_subtract_fusion
  (1 shorter events, 0.0 us)
Async XLA Ops:
  7.2 42.1 %all-gather.2.cloned.1.call-start = ((), (), s32[]{:S(2)}) async-start(), calls=%async_computation.2 | async-start | bytes 2228224 | tf_op jit(solution)/shard_map/all_gather | solution.py:35
  8.9 135.3 %reduce-scatter.3.cloned.1.call-start = ((), (), s32[]{:S(2)}) async-start(), calls=%async_computation.3 | async-start | bytes 1179648 | tf_op jit(solution)/shard_map/reduce_scatter | solution.py:52
  9.8 39.4 %copy-start.6 = (s32[1,1,2048]{2,1,0:T(1,128)S(1)}, s32[1,1,2048]{2,1,0:T(1,128)}, u32[]{:S(2)}) copy-start(s32[1,1,2048]{2,1,0:T(1,128)} %param.12) | copy-start | bytes 24580
  49.2 9.5 %copy-start.4 = (bf16[4096,256]{1,0:T(8,128)(2,1)S(1)}, bf16[4096,256]{1,0:T(8,128)(2,1)}, u32[]{:S(2)}) copy-start(bf16[4096,256]{1,0:T(8,128)(2,1)} %all-gather.2.cloned.1.call-done) | copy-start | bytes 6291460
  49.2 9.5 %copy-start.7 = (s32[1,1024]{1,0:T(1,128)S(1)}, s32[1,1024]{1,0:T(1,128)}, u32[]{:S(2)}) copy-start(s32[1,1024]{1,0:T(1,128)} %param.13) | copy-start | bytes 12292
  61.6 4.5 %copy-start.5 = (s32[1,1,2048]{2,1,0:T(1,128)S(1)}, s32[1,1,2048]{2,1,0:T(1,128)}, u32[]{:S(2)}) copy-start(s32[1,1,2048]{2,1,0:T(1,128)} %param.11) | copy-start | bytes 24580
  72.1 143.3 %reduce-scatter.5.cloned.1.call-start = ((), (), s32[]{:S(2)}) async-start(), calls=%async_computation.4 | async-start | bytes 4456448 | tf_op jit(solution)/shard_map/reduce_scatter | solution.py:58
  87.0 58.2 %copy-start.3 = (f32[128]{0:T(128)S(1)}, f32[128]{0:T(128)}, u32[]{:S(2)}) copy-start(f32[128]{0:T(128)} %param.8) | copy-start | bytes 1540
  87.0 58.7 %copy-start.1 = (f32[128,256]{1,0:T(8,128)S(1)}, f32[128,256]{1,0:T(8,128)}, u32[]{:S(2)}) copy-start(f32[128,256]{1,0:T(8,128)} %param.7) | copy-start | bytes 393220
  87.0 129.5 %copy-start.2 = (f32[256]{0:T(256)S(1)}, f32[256]{0:T(256)}, u32[]{:S(2)}) copy-start(f32[256]{0:T(256)} %param.10) | copy-start | bytes 3076
  87.0 130.1 %copy-start = (f32[256,256]{1,0:T(8,128)S(1)}, f32[256,256]{1,0:T(8,128)}, u32[]{:S(2)}) copy-start(f32[256,256]{1,0:T(8,128)} %param.9) | copy-start | bytes 786436
Sparse Core Ops, SparseCore 0:
  10.3 38.9 all-gather.1
  72.3 71.9 reduce-scatter.2
  146.7 68.6 reduce-scatter.4
where the time goes:
time: 227 us; the launch traced here: 225 us
  waiting for transfers between devices  131 us (58%)
  matrix products  40.6 us (18%)
  blocking collectives  30.4 us (13%)
  between operations  13.9 us (6%)
  other arithmetic  9.11 us (4%)
    reduce_scatter x1, waiting for transfers between devices, per_device(): lax.psum_scatter(spread_rows(item_index, item_grad, item_owned * lax.axis...  68.1 us
    reduce_scatter x1, waiting for transfers between devices, per_device(): lax.psum_scatter(spread_rows(user_index, user_grad, user_owned * lax.axis...  57.2 us
    all_gather x1, blocking collectives, per_device(): lax.all_gather(user_table.astype(jnp.bfloat16), 'item', axis=0, tiled=True)  30.4 us
    dot_general x3, matrix products, spread_rows(): return jnp.dot(one_hot, values, preferred_element_type=jnp.float32)  17.3 us
    dot_general x3, matrix products, take_rows(): return jnp.dot(one_hot, shard_rows, preferred_element_type=jnp.float32)  15.3 us
    all_gather x1, waiting for transfers between devices, per_device(): lax.all_gather(item_table.astype(jnp.bfloat16), 'user', axis=0, tiled=True)  5.99 us
  transfers between devices with their start and end apart: 3, of which 3 were waited for; matrix products, arithmetic and copies ran while one was open for 10% of the time, Pallas kernels for 0%

commit v1 on v0

v1 whole, which is shorter than its diff:
```python
import jax
import jax.numpy as jnp
from jax import lax
from jax.experimental import pallas as pl
from jax.experimental.pallas import tpu as pltpu
from jax.sharding import PartitionSpec as P

learn_rate = 0.1
MESH = pl.DeviceIdType.MESH
BF = jnp.bfloat16
F32 = jnp.float32

D = 256
EDGES = 2048
NEG = 1024
PICKS = EDGES + NEG
UR = 128
IR = 256
PLANE = 4 * IR
BLK = 256


def one_hot_cols(index, width):
    lane = lax.broadcasted_iota(jnp.int32, index.shape, 1)
    parts = [
        jnp.where(index == lane + 128 * c, F32(1), F32(0)).astype(BF) for c in range(width // 128)
    ]
    return jnp.concatenate(parts, axis=1)


def one_hot_rows(index, base, rows):
    row = lax.broadcasted_iota(jnp.int32, (rows, index.shape[1]), 0) + base
    return jnp.where(row == index, F32(1), F32(0)).astype(BF)


def to_column(row):
    return jnp.broadcast_to(row, (128, 128)).T


def adagrad(table, state_ref, total, out_ref, out_state_ref):
    rows = total.shape[0]
    mean = jnp.sum(total * total, axis=1, keepdims=True) * (1.0 / D)
    for b in range(rows // 128):
        part = slice(128 * b, 128 * (b + 1))
        new_state = to_column(state_ref[:, part]) + mean[part]
        out_state_ref[:, part] = new_state.T[0:1, :]
        scale = learn_rate / jnp.sqrt(new_state)
        out_ref[part, :] = table[part, :] - total[part] * jnp.concatenate([scale, scale], axis=1)


def kernel(
    user_table, user_state, item_table, item_state, edge_users, edge_items, negatives,
    new_user_table, new_user_state, new_item_table, new_item_state,
    items, users, user_col, item_col, item_row, picked, picked_users, picked_negs, neg_grad,
    user_grad, item_grad,
    user_keep, u2s, u2r, uzs, uzr, uys, uyr,
    plane_sum, keep, sib_s, sib_r, z2s, z2r, zs, zr, ys, yr,
    send_sem, recv_sem,
):
    u, t = lax.axis_index("user"), lax.axis_index("item")
    k, yl, z = lax.rem(u, 2), lax.rem(lax.div(u, 2), 2), lax.div(u, 4)
    yh, x = lax.rem(t, 2), lax.div(t, 2)

    def user_id(zz, yy, kk):
        return (zz * 2 + yy) * 2 + kk

    def item_id(xx, yy):
        return xx * 2 + yy

    zp, zm, z2 = lax.rem(z + 1, 4), lax.rem(z + 3, 4), lax.rem(z + 2, 4)
    xp, xm, x2 = lax.rem(x + 1, 4), lax.rem(x + 3, 4), lax.rem(x + 2, 4)
    sib = {"user": user_id(z, yl, 1 - k)}
    yn = {"user": user_id(z, 1 - yl, k)}
    zup = {"user": user_id(zp, yl, k)}
    zdn = {"user": user_id(zm, yl, k)}
    hn = {"item": item_id(x, 1 - yh)}
    xup = {"item": item_id(xp, yh)}
    xdn = {"item": item_id(xm, yh)}

    barrier = pltpu.get_barrier_semaphore()
    for peer in (sib, yn, zup, zdn, hn, xup, xdn):
        pl.semaphore_signal(barrier, inc=1, device_id=peer, device_id_type=MESH)

    copies = []

    def message(src, dst, peer):
        n = len(copies)
        copy = pltpu.make_async_remote_copy(
            src_ref=src, dst_ref=dst, send_sem=send_sem.at[n], recv_sem=recv_sem.at[n],
            device_id=peer, device_id_type=MESH,
        )
        copies.append(copy)
        return copy

    def send(src, dst, peer):
        copy = message(src, dst, peer)
        copy.start()
        return copy

    items[u] = item_table[...].astype(BF)
    users[t] = user_table[...].astype(BF)
    pl.semaphore_wait(barrier, 7)

    def slot(ref, s):
        return ref.at[s]

    own_i, own_u = slot(items, u), slot(users, t)
    m_zup = send(own_i, own_i, zup)
    m_zdn = send(own_i, own_i, zdn)
    m_yn = send(own_i, own_i, yn)
    m_sib = send(own_i, own_i, sib)
    m_xup = send(own_u, own_u, xup)
    m_xdn = send(own_u, own_u, xdn)
    m_hn = send(own_u, own_u, hn)

    for b in range(EDGES // 128):
        part = slice(128 * b, 128 * (b + 1))
        user_col[part, :] = to_column(edge_users[0, :, part])
        item_col[part, :] = to_column(edge_items[0, :, part])
    for b in range(NEG // 128):
        item_col[EDGES + 128 * b:EDGES + 128 * (b + 1), :] = to_column(
            negatives[:, 128 * b:128 * (b + 1)]
        )
    item_row[:, :EDGES] = edge_items[0, :, :]
    item_row[:, EDGES:] = negatives[...]

    def pick_plane(zz, first):
        @pl.loop(0, PICKS // BLK)
        def _(b):
            rows = pl.ds(pl.multiple_of(b * BLK, BLK), BLK)
            one_hot = one_hot_cols(item_col[rows, :] - zz * PLANE, PLANE)
            plane = items[pl.ds(zz * 4, 4)].reshape(PLANE, D)
            got = jnp.dot(one_hot, plane, preferred_element_type=F32)
            picked[rows, :] = got if first else picked[rows, :] + got

    m_zup.wait_recv()
    s_zm = slot(items, user_id(zm, yl, k))
    lo, hi = pl.ds(0, IR // 2), pl.ds(IR // 2, IR // 2)
    m_z2a = send(s_zm.at[lo], s_zm.at[lo], zup)
    f_zm = send(s_zm, s_zm, sib)
    m_zdn.wait_recv()
    s_zp = slot(items, user_id(zp, yl, k))
    m_z2b = send(s_zp.at[hi], s_zp.at[hi], zdn)
    f_zp = send(s_zp, s_zp, sib)
    m_yn.wait_recv()
    s_yn = slot(items, user_id(z, 1 - yl, k))
    m_yzup = send(s_yn, s_yn, zup)
    m_yzdn = send(s_yn, s_yn, zdn)
    f_yn = send(s_yn, s_yn, sib)

    ulo, uhi = pl.ds(0, UR // 2), pl.ds(UR // 2, UR // 2)
    m_hn.wait_recv()
    s_hn = slot(users, item_id(x, 1 - yh))
    m_hxup = send(s_hn, s_hn, xup)
    m_hxdn = send(s_hn, s_hn, xdn)
    m_xup.wait_recv()
    s_xm = slot(users, item_id(xm, yh))
    m_x2a = send(s_xm.at[ulo], s_xm.at[ulo], xup)
    m_xdn.wait_recv()
    s_xp = slot(users, item_id(xp, yh))
    m_x2b = send(s_xp.at[uhi], s_xp.at[uhi], xdn)

    m_sib.wait_recv()
    f_yn.wait_recv()
    pick_plane(z, True)

    m_z2a.wait_recv()
    m_z2b.wait_recv()
    s_z2 = slot(items, user_id(z2, yl, k))
    m_z2y = send(s_z2, s_z2, yn)
    f_z2 = send(s_z2, s_z2, sib)
    m_hxup.wait_recv()
    s_hxm = slot(users, item_id(xm, 1 - yh))
    m_hx2a = send(s_hxm.at[ulo], s_hxm.at[ulo], xup)
    m_hxdn.wait_recv()
    s_hxp = slot(users, item_id(xp, 1 - yh))
    m_hx2b = send(s_hxp.at[uhi], s_hxp.at[uhi], xdn)

    m_yzup.wait_recv()
    s_yzm = slot(items, user_id(zm, 1 - yl, k))
    f_yzm = send(s_yzm, s_yzm, sib)
    m_yzdn.wait_recv()
    s_yzp = slot(items, user_id(zp, 1 - yl, k))
    f_yzp = send(s_yzp, s_yzp, sib)
    f_zm.wait_recv()
    f_yzm.wait_recv()
    pick_plane(zm, False)
    m_z2y.wait_recv()
    s_z2y = slot(items, user_id(z2, 1 - yl, k))
    f_z2y = send(s_z2y, s_z2y, sib)
    f_zp.wait_recv()
    f_yzp.wait_recv()
    pick_plane(zp, False)

    m_x2a.wait_recv()
    m_x2b.wait_recv()
    m_hx2a.wait_recv()
    m_hx2b.wait_recv()

    @pl.loop(0, EDGES // BLK)
    def _(b):
        rows = pl.ds(pl.multiple_of(b * BLK, BLK), BLK)
        one_hot = one_hot_cols(user_col[rows, :], 8 * UR)
        got = jnp.dot(one_hot, users[...].reshape(8 * UR, D), preferred_element_type=F32)
        picked_users[rows, :] = got.astype(BF)

    f_z2.wait_recv()
    f_z2y.wait_recv()
    pick_plane(z2, False)

    picked_negs[...] = picked[EDGES:, :].astype(BF)
    neg_grad[...] = jnp.zeros_like(neg_grad)

    @pl.loop(0, EDGES // BLK)
    def _(b):
        rows = pl.ds(pl.multiple_of(b * BLK, BLK), BLK)
        mine = picked_users[rows, :]
        wide = mine.astype(F32)
        item = picked[rows, :]
        negs = picked_negs[...]
        positive = jnp.sum(wide * item, axis=1, keepdims=True)
        pull = jax.nn.sigmoid(-positive)
        scores = lax.dot_general(mine, negs, (((1,), (1,)), ((), ())), preferred_element_type=F32)
        weights = (jax.nn.sigmoid(scores) * (1.0 / NEG)).astype(BF)
        user_grad[rows, :] = (
            -pull * item + jnp.dot(weights, negs, preferred_element_type=F32)
        ).astype(BF)
        item_grad[rows, :] = (-pull * wide).astype(BF)
        neg_grad[...] += lax.dot_general(
            weights, mine, (((0,), (0,)), ((), ())), preferred_element_type=F32
        )

    item_grad[EDGES:, :] = neg_grad[...].astype(BF)

    def spread_users(xx):
        one_hot = one_hot_rows(edge_users[0, :, :], xx * (2 * UR), 2 * UR)
        return jnp.dot(one_hot, user_grad[...], preferred_element_type=F32)

    got = spread_users(x2).astype(BF)
    u2s[...] = got.reshape(2, UR, D)
    m_u2p = send(u2s.at[0], u2r.at[0], xup)
    m_u2m = send(u2s.at[1], u2r.at[1], xdn)
    for n, xx in enumerate((xp, xm, x)):
        user_keep[n] = spread_users(xx).reshape(2, UR, D)

    def spread_items(zz, n):
        for m in range(4):
            @pl.loop(0, PICKS // 512)
            def _(c, m=m):
                part = pl.ds(pl.multiple_of(c * 512, 512), 512)
                one_hot = one_hot_rows(item_row[:, part], zz * PLANE + m * IR, IR)
                got = jnp.dot(one_hot, item_grad[part, :], preferred_element_type=F32)
                plane_sum[m] = jnp.where(c == 0, got, plane_sum[m] + got)
        for yy in range(2):
            sib_s[n, yy] = plane_sum[2 * yy + 1 - k].astype(BF)
            keep[n, yy] = plane_sum[2 * yy + k]
        return send(sib_s.at[n], sib_r.at[n], sib)

    m_s0 = spread_items(z2, 0)

    m_u2p.wait_recv()
    m_u2m.wait_recv()
    uzs[0, 0] = (user_keep[0, 0] + u2r[0].astype(F32)).astype(BF)
    uzs[0, 1] = user_keep[0, 1].astype(BF)
    m_uzp = send(uzs.at[0], uzr.at[0], xup)
    uzs[1, 0] = user_keep[1, 0].astype(BF)
    uzs[1, 1] = (user_keep[1, 1] + u2r[1].astype(F32)).astype(BF)
    m_uzm = send(uzs.at[1], uzr.at[1], xdn)

    m_s0.wait_recv()
    z2s[...] = (keep[0] + sib_r[0].astype(F32)).astype(BF)
    m_z2p = send(z2s.at[0], z2r.at[0], zup)
    m_z2m = send(z2s.at[1], z2r.at[1], zdn)

    m_s1 = spread_items(zp, 1)
    m_s2 = spread_items(zm, 2)

    m_s1.wait_recv()
    m_z2p.wait_recv()
    zs[0, 0] = (keep[1, 0] + sib_r[1, 0].astype(F32) + z2r[0].astype(F32)).astype(BF)
    zs[0, 1] = (keep[1, 1] + sib_r[1, 1].astype(F32)).astype(BF)
    m_zp = send(zs.at[0], zr.at[0], zup)
    m_s2.wait_recv()
    m_z2m.wait_recv()
    zs[1, 0] = (keep[2, 0] + sib_r[2, 0].astype(F32)).astype(BF)
    zs[1, 1] = (keep[2, 1] + sib_r[2, 1].astype(F32) + z2r[1].astype(F32)).astype(BF)
    m_zm = send(zs.at[1], zr.at[1], zdn)

    m_s3 = spread_items(z, 3)

    m_uzp.wait_recv()
    m_uzm.wait_recv()
    user_keep[2] = user_keep[2] + uzr[0].astype(F32) + uzr[1].astype(F32)
    uys[...] = user_keep[2, 1 - yh].astype(BF)
    m_uy = send(uys, uyr, hn)

    m_s3.wait_recv()
    keep[3] = keep[3] + sib_r[3].astype(F32)
    m_zp.wait_recv()
    m_zm.wait_recv()
    ys[...] = (keep[3, 1 - yl] + zr[0, 1 - yl].astype(F32) + zr[1, 1 - yl].astype(F32)).astype(BF)
    m_y = send(ys, yr, yn)
    keep[3, yl] = keep[3, yl] + zr[0, yl].astype(F32) + zr[1, yl].astype(F32)

    m_uy.wait_recv()
    adagrad(
        user_table, user_state, user_keep[2, yh] + uyr[...].astype(F32),
        new_user_table, new_user_state,
    )
    m_y.wait_recv()
    adagrad(
        item_table, item_state, keep[3, yl] + yr[...].astype(F32), new_item_table, new_item_state
    )
    for copy in copies:
        copy.wait_send()


MESSAGES = 40


def per_device(user_table, user_state, item_table, item_state, edge_users, edge_items, negatives):
    vmem = pl.BlockSpec(memory_space=pltpu.VMEM)
    scratch = [
        ((16, IR, D), BF),
        ((8, UR, D), BF),
        ((EDGES, 128), jnp.int32),
        ((PICKS, 128), jnp.int32),
        ((1, PICKS), jnp.int32),
        ((PICKS, D), F32),
        ((EDGES, D), BF),
        ((NEG, D), BF),
        ((NEG, D), F32),
        ((EDGES, D), BF),
        ((PICKS, D), BF),
        ((3, 2, UR, D), F32),
        ((2, UR, D), BF),
        ((2, UR, D), BF),
        ((2, 2, UR, D), BF),
        ((2, 2, UR, D), BF),
        ((UR, D), BF),
        ((UR, D), BF),
        ((4, IR, D), F32),
        ((4, 2, IR, D), F32),
        ((4, 2, IR, D), BF),
        ((4, 2, IR, D), BF),
        ((2, IR, D), BF),
        ((2, IR, D), BF),
        ((2, 2, IR, D), BF),
        ((2, 2, IR, D), BF),
        ((IR, D), BF),
        ((IR, D), BF),
    ]
    out = pl.pallas_call(
        kernel,
        out_shape=[
            jax.ShapeDtypeStruct((UR, D), F32),
            jax.ShapeDtypeStruct((1, UR), F32),
            jax.ShapeDtypeStruct((IR, D), F32),
            jax.ShapeDtypeStruct((1, IR), F32),
        ],
        in_specs=[vmem] * 7,
        out_specs=[vmem] * 4,
        scratch_shapes=[pltpu.VMEM(shape, kind) for shape, kind in scratch]
        + [pltpu.SemaphoreType.DMA((MESSAGES,)), pltpu.SemaphoreType.DMA((MESSAGES,))],
        compiler_params=pltpu.CompilerParams(
            collective_id=0, has_side_effects=True, vmem_limit_bytes=48 * 1024 * 1024
        ),
        name="step",
    )(
        user_table, user_state.reshape(1, UR), item_table, item_state.reshape(1, IR),
        edge_users, edge_items, negatives,
    )
    return (out[0], out[1].reshape(UR), out[2], out[3].reshape(IR))


def solution(mesh):
    in_specs = (
        P(("user", "item"), None),
        P(("user", "item")),
        P(("item", "user"), None),
        P(("item", "user")),
        P("user", "item", None),
        P("user", "item", None),
        P("item", None),
    )
    out_specs = (
        P(("user", "item"), None),
        P(("user", "item")),
        P(("item", "user"), None),
        P(("item", "user")),
    )
    return jax.shard_map(
        per_device, mesh=mesh, in_specs=in_specs, out_specs=out_specs, check_vma=False
    )
```

time: 227 us -> 82.8 us (0.36)
  waiting for transfers between devices: 131 us -> 0 us
  Pallas kernels: 0 us -> 74.8 us
  matrix products: 40.6 us -> 0 us
  blocking collectives: 30.4 us -> 0 us
  between operations: 13.9 us -> 0.66 us
  other arithmetic: 9.11 us -> 0 us
  local copies, waits for them, and re-layouts: 0.03 us -> 7.03 us
    reduce_scatter x2 -> x0, waiting for transfers between devices: 125 us -> none  [the longest x1 68.1 us: per_device(): lax.psum_scatter(spread_rows(item_index, item_grad, item_owned * lax.axis...]
    pallas_call x0 -> x1, Pallas kernels: none -> 74.8 us  [per_device(): pl.pallas_call(kernel, out_shape=[jax.ShapeDtypeStruct((UR, D), F32), jax...]
    dot_general x8 -> x0, matrix products: 40.6 us -> none  [the longest x3 17.3 us: spread_rows(): return jnp.dot(one_hot, values, preferred_element_type=jnp.float32)]
    all_gather x1 -> x0, blocking collectives: 30.4 us -> none  [per_device(): lax.all_gather(user_table.astype(jnp.bfloat16), 'item', axis=0, tiled=True)]
    unnamed x16 -> x18, local copies, waits for them, and re-layouts: 0.03 us -> 7.03 us
    all_gather x1 -> x0, waiting for transfers between devices: 5.99 us -> none  [per_device(): lax.all_gather(item_table.astype(jnp.bfloat16), 'user', axis=0, tiled=True)]
    sub x2 -> x0, other arithmetic: 3.41 us -> none  [adagrad(): table - learn_rate * gradient / jnp.sqrt(new_state)[:, None]]
    convert_element_type x2 -> x0, other arithmetic: 2.54 us -> none  [the longest x1 1.62 us: per_device(): item_table.astype(jnp.bfloat16)]
  transfers between devices with their start and end apart: 3 -> 0, of which waited for: 3 -> 0; matrix products, arithmetic and copies ran while one was open for 10% -> 0% of each run, Pallas kernels for 0% -> 0%
where the time goes in v1:
time: 82.8 us; the launch traced here: 82.5 us
  Pallas kernels  74.8 us (90%)
  local copies, waits for them, and re-layouts  7.03 us (8%)
    pallas_call x1, Pallas kernels, per_device(): pl.pallas_call(kernel, out_shape=[jax.ShapeDtypeStruct((UR, D), F32), jax...  74.8 us
    unnamed x18, local copies, waits for them, and re-layouts  7.03 us

profile of v1, /device:TPU:1, one launch (start us, length us, event | category | flops | bytes accessed | tf_op | source)
XLA Modules:
  0.0 82.5 jit_solution(15658549038077748938)
XLA Ops:
  0.6 0.0 copy-start.5
  0.6 0.0 copy-start.6
  0.7 0.7 copy-done.5
  1.3 0.0 copy-done.6
  1.3 0.0 copy-start
  1.3 0.9 %copy-done = f32[256,256]{1,0:T(8,128)S(1)} copy-done((f32[256,256]{1,0:T(8,128)S(1)}, f32[256,256]{1,0:T(8,128)}, u32[]{:S(2)}) %copy-start) | copy-done | bytes 262168
  2.3 0.0 copy-start.1
  2.3 0.9 %copy-done.1 = f32[128,256]{1,0:T(8,128)S(1)} copy-done((f32[128,256]{1,0:T(8,128)S(1)}, f32[128,256]{1,0:T(8,128)}, u32[]{:S(2)}) %copy-start.1) | copy-done | bytes 131096
  3.2 0.0 copy-start.2
  3.2 0.7 copy-done.2
  3.9 0.0 copy-start.3
  3.9 0.7 copy-done.3
  4.6 0.0 copy-start.4
  4.6 0.7 copy-done.4
  5.3 74.8 %step.1 = (f32[128,256]{1,0:T(8,128)S(1)}, f32[1,128]{1,0:T(1,128)S(1)}, f32[256,256]{1,0:T(8,128)S(1)}, f32[1,256]{1,0:T(1,128)S(1)}) custom-call(f32[128,256]{1,0:T(8,128)S(1)} %copy-done.1, f32[1,128]{1,0:T(1,128)S(1)} %bitcast.6, f32[256,256]{1,0:T(8,128)S(1)} %copy-done, f32[1,256]{1,0:T(1,128)S(1)} %bitcast.4, s32[1,1,2048]{2,1,0:T(1,128)S(1)} %copy-done.2, ...), custom_call_target="tpu_custom_call" | custom-call | tf_op jit(solution)/shard_map/step/pallas_call | solution.py:353
  80.1 0.7 copy.15
  80.7 0.5 copy.16
  81.2 0.7 copy.17
  81.9 0.6 copy.18
Async XLA Ops:
  0.6 0.7 copy-start.5
  0.6 0.7 copy-start.6
  1.3 1.0 %copy-start = (f32[256,256]{1,0:T(8,128)S(1)}, f32[256,256]{1,0:T(8,128)}, u32[]{:S(2)}) copy-start(f32[256,256]{1,0:T(8,128)} %item_table.1) | copy-start | bytes 786436
  2.3 0.9 %copy-start.1 = (f32[128,256]{1,0:T(8,128)S(1)}, f32[128,256]{1,0:T(8,128)}, u32[]{:S(2)}) copy-start(f32[128,256]{1,0:T(8,128)} %user_table.1) | copy-start | bytes 393220
  3.2 0.7 copy-start.2
  3.9 0.7 copy-start.3
  4.6 0.7 copy-start.4

commit v2 on v1

--- a/solution.py
+++ b/solution.py
@@ -17,7 +17,7 @@
 UR = 128
 IR = 256
 PLANE = 4 * IR
-BLK = 256
+BLK = 512
 
 
 def one_hot_cols(index, width):
@@ -49,8 +49,9 @@
 
 
 def kernel(
-    user_table, user_state, item_table, item_state, edge_users, edge_items, negatives,
+    user_table_h, user_state_h, item_table_h, item_state_h, edge_users_h, edge_items_h, negatives_h,
     new_user_table, new_user_state, new_item_table, new_item_state,
+    user_table, user_state, item_table, item_state, edge_users, edge_items, negatives, load_sem,
     items, users, user_col, item_col, item_row, picked, picked_users, picked_negs, neg_grad,
     user_grad, item_grad,
     user_keep, u2s, u2r, uzs, uzr, uys, uyr,
@@ -77,6 +78,17 @@
     xup = {"item": item_id(xp, yh)}
     xdn = {"item": item_id(xm, yh)}
 
+    pairs = (
+        (item_table_h, item_table), (user_table_h, user_table), (edge_users_h, edge_users),
+        (edge_items_h, edge_items), (negatives_h, negatives),
+        (user_state_h, user_state), (item_state_h, item_state),
+    )
+    loads = [
+        pltpu.make_async_copy(src, dst, load_sem.at[n]) for n, (src, dst) in enumerate(pairs)
+    ]
+    for load in loads:
+        load.start()
+
     barrier = pltpu.get_barrier_semaphore()
     for peer in (sib, yn, zup, zdn, hn, xup, xdn):
         pl.semaphore_signal(barrier, inc=1, device_id=peer, device_id_type=MESH)
@@ -97,7 +109,9 @@
         copy.start()
         return copy
 
+    loads[0].wait()
     items[u] = item_table[...].astype(BF)
+    loads[1].wait()
     users[t] = user_table[...].astype(BF)
     pl.semaphore_wait(barrier, 7)
 
@@ -113,6 +127,8 @@
     m_xdn = send(own_u, own_u, xdn)
     m_hn = send(own_u, own_u, hn)
 
+    for load in loads[2:]:
+        load.wait()
     for b in range(EDGES // 128):
         part = slice(128 * b, 128 * (b + 1))
         user_col[part, :] = to_column(edge_users[0, :, part])
@@ -125,11 +141,10 @@
     item_row[:, EDGES:] = negatives[...]
 
     def pick_plane(zz, first):
-        @pl.loop(0, PICKS // BLK)
-        def _(b):
-            rows = pl.ds(pl.multiple_of(b * BLK, BLK), BLK)
+        plane = items[pl.ds(zz * 4, 4)].reshape(PLANE, D)
+        for b in range(PICKS // BLK):
+            rows = pl.ds(b * BLK, BLK)
             one_hot = one_hot_cols(item_col[rows, :] - zz * PLANE, PLANE)
-            plane = items[pl.ds(zz * 4, 4)].reshape(PLANE, D)
             got = jnp.dot(one_hot, plane, preferred_element_type=F32)
             picked[rows, :] = got if first else picked[rows, :] + got
 
@@ -197,9 +212,8 @@
     m_hx2a.wait_recv()
     m_hx2b.wait_recv()
 
-    @pl.loop(0, EDGES // BLK)
-    def _(b):
-        rows = pl.ds(pl.multiple_of(b * BLK, BLK), BLK)
+    for b in range(EDGES // BLK):
+        rows = pl.ds(b * BLK, BLK)
         one_hot = one_hot_cols(user_col[rows, :], 8 * UR)
         got = jnp.dot(one_hot, users[...].reshape(8 * UR, D), preferred_element_type=F32)
         picked_users[rows, :] = got.astype(BF)
@@ -211,9 +225,8 @@
     picked_negs[...] = picked[EDGES:, :].astype(BF)
     neg_grad[...] = jnp.zeros_like(neg_grad)
 
-    @pl.loop(0, EDGES // BLK)
-    def _(b):
-        rows = pl.ds(pl.multiple_of(b * BLK, BLK), BLK)
+    for b in range(EDGES // BLK):
+        rows = pl.ds(b * BLK, BLK)
         mine = picked_users[rows, :]
         wide = mine.astype(F32)
         item = picked[rows, :]
@@ -245,12 +258,8 @@
 
     def spread_items(zz, n):
         for m in range(4):
-            @pl.loop(0, PICKS // 512)
-            def _(c, m=m):
-                part = pl.ds(pl.multiple_of(c * 512, 512), 512)
-                one_hot = one_hot_rows(item_row[:, part], zz * PLANE + m * IR, IR)
-                got = jnp.dot(one_hot, item_grad[part, :], preferred_element_type=F32)
-                plane_sum[m] = jnp.where(c == 0, got, plane_sum[m] + got)
+            one_hot = one_hot_rows(item_row[...], zz * PLANE + m * IR, IR)
+            plane_sum[m] = jnp.dot(one_hot, item_grad[...], preferred_element_type=F32)
         for yy in range(2):
             sib_s[n, yy] = plane_sum[2 * yy + 1 - k].astype(BF)
             keep[n, yy] = plane_sum[2 * yy + k]
@@ -318,8 +327,24 @@
 MESSAGES = 40
 
 
+def store(*refs):
+    sources, targets, sem = refs[:4], refs[4:8], refs[8]
+    moves = [
+        pltpu.make_async_copy(a, b, sem.at[n]) for n, (a, b) in enumerate(zip(sources, targets))
+    ]
+    for move in moves:
+        move.start()
+    for move in moves:
+        move.wait()
+
+
 def per_device(user_table, user_state, item_table, item_state, edge_users, edge_items, negatives):
     vmem = pl.BlockSpec(memory_space=pltpu.VMEM)
+    hbm = pl.BlockSpec(memory_space=pltpu.HBM)
+    local = [
+        ((UR, D), F32), ((1, UR), F32), ((IR, D), F32), ((1, IR), F32),
+        ((1, 1, EDGES), jnp.int32), ((1, 1, EDGES), jnp.int32), ((1, NEG), jnp.int32),
+    ]
     scratch = [
         ((16, IR, D), BF),
         ((8, UR, D), BF),
@@ -350,26 +375,37 @@
         ((IR, D), BF),
         ((IR, D), BF),
     ]
+    shapes = [jax.ShapeDtypeStruct(shape, kind) for shape, kind in local[:4]]
     out = pl.pallas_call(
         kernel,
-        out_shape=[
-            jax.ShapeDtypeStruct((UR, D), F32),
-            jax.ShapeDtypeStruct((1, UR), F32),
-            jax.ShapeDtypeStruct((IR, D), F32),
-            jax.ShapeDtypeStruct((1, IR), F32),
-        ],
-        in_specs=[vmem] * 7,
+        out_shape=[pltpu.VMEM(shape, kind) for shape, kind in local[:4]],
+        in_specs=[hbm] * 7,
         out_specs=[vmem] * 4,
-        scratch_shapes=[pltpu.VMEM(shape, kind) for shape, kind in scratch]
+        scratch_shapes=[pltpu.VMEM(shape, kind) for shape, kind in local]
+        + [pltpu.SemaphoreType.DMA((7,))]
+        + [pltpu.VMEM(shape, kind) for shape, kind in scratch]
         + [pltpu.SemaphoreType.DMA((MESSAGES,)), pltpu.SemaphoreType.DMA((MESSAGES,))],
         compiler_params=pltpu.CompilerParams(
             collective_id=0, has_side_effects=True, vmem_limit_bytes=48 * 1024 * 1024
         ),
         name="step",
     )(
-        user_table, user_state.reshape(1, UR), item_table, item_state.reshape(1, IR),
-        edge_users, edge_items, negatives,
-    )
+        *(
+            pltpu.with_memory_space_constraint(a, pltpu.HBM)
+            for a in (
+                user_table, user_state.reshape(1, UR), item_table, item_state.reshape(1, IR),
+                edge_users, edge_items, negatives,
+            )
+        )
+    )
+    out = pl.pallas_call(
+        store,
+        out_shape=shapes,
+        in_specs=[vmem] * 4,
+        out_specs=[hbm] * 4,
+        scratch_shapes=[pltpu.SemaphoreType.DMA((4,))],
+        name="store",
+    )(*out)
     return (out[0], out[1].reshape(UR), out[2], out[3].reshape(IR))
 
 

time: 82.8 us -> 56.8 us (0.69)
  the two profiles are of different devices: /device:TPU:1 before, /device:TPU:6 now
where the time goes in v2:
time: 56.8 us; the launch traced here: 56.7 us
  Pallas kernels  53.9 us (95%)
  local copies, waits for them, and re-layouts  1.9 us (3%)
  between operations  0.81 us (1%)
    pallas_call x1, Pallas kernels, per_device(): pl.pallas_call(kernel, out_shape=[pltpu.VMEM(shape, kind) for shape, kind...  52.1 us
    unnamed x8, local copies, waits for them, and re-layouts  1.9 us
    pallas_call x1, Pallas kernels, per_device(): pl.pallas_call(store, out_shape=shapes, in_specs=[vmem] * 4, out_specs=[h...  1.81 us

profile of v2, /device:TPU:6, one launch (start us, length us, event | category | flops | bytes accessed | tf_op | source)
XLA Modules:
  0.0 56.7 jit_solution(17643426091208117381)
XLA Ops:
  0.6 52.1 %step.1 = (f32[128,256]{1,0:T(8,128)S(1)}, f32[1,128]{1,0:T(1,128)S(1)}, f32[256,256]{1,0:T(8,128)S(1)}, f32[1,256]{1,0:T(1,128)S(1)}) custom-call(f32[128,256]{1,0:T(8,128)} %user_table_h.1, f32[1,128]{1,0:T(1,128)} %bitcast.5, f32[256,256]{1,0:T(8,128)} %item_table_h.1, f32[1,256]{1,0:T(1,128)} %bitcast.4, s32[1,1,2048]{2,1,0:T(1,128)} %edge_users_h.1, ...), custom_call_target="tpu_custom_call" | custom-call | tf_op jit(solution)/shard_map/step/pallas_call | solution.py:379
  52.8 0.0 copy-start
  52.8 0.7 %copy-done = f32[256,256]{1,0:T(8,128)} copy-done((f32[256,256]{1,0:T(8,128)}, f32[256,256]{1,0:T(8,128)S(1)}, u32[]{:S(2)}) %copy-start) | copy-done | bytes 262168
  53.5 0.0 copy-start.1
  53.5 0.6 %copy-done.1 = f32[128,256]{1,0:T(8,128)} copy-done((f32[128,256]{1,0:T(8,128)}, f32[128,256]{1,0:T(8,128)S(1)}, u32[]{:S(2)}) %copy-start.1) | copy-done | bytes 131096
  54.1 0.0 copy-start.3
  54.1 0.0 copy-start.2
  54.1 0.5 copy-done.3
  54.7 0.0 copy-done.2
  54.7 1.8 %store.1 = (f32[128,256]{1,0:T(8,128)}, f32[1,128]{1,0:T(1,128)}, f32[256,256]{1,0:T(8,128)}, f32[1,256]{1,0:T(1,128)}) custom-call(f32[128,256]{1,0:T(8,128)} %copy-done.1, f32[1,128]{1,0:T(1,128)} %copy-done.3, f32[256,256]{1,0:T(8,128)} %copy-done, f32[1,256]{1,0:T(1,128)} %copy-done.2), custom_call_target="tpu_custom_call" | custom-call | tf_op jit(solution)/shard_map/store/pallas_call | solution.py:401
Async XLA Ops:
  52.8 0.7 %copy-start = (f32[256,256]{1,0:T(8,128)}, f32[256,256]{1,0:T(8,128)S(1)}, u32[]{:S(2)}) copy-start(f32[256,256]{1,0:T(8,128)S(1)} %get-tuple-element.14.refs_2_) | copy-start | bytes 786436
  53.5 0.6 %copy-start.1 = (f32[128,256]{1,0:T(8,128)}, f32[128,256]{1,0:T(8,128)S(1)}, u32[]{:S(2)}) copy-start(f32[128,256]{1,0:T(8,128)S(1)} %get-tuple-element.12.refs_0_) | copy-start | bytes 393220
  54.1 0.5 copy-start.3
  54.1 0.6 copy-start.2

commit v3 on v0

v3 whole, which is shorter than its diff:
```python
import jax
import jax.numpy as jnp
from jax import lax
from jax.experimental import pallas as pl
from jax.experimental.pallas import tpu as pltpu
from jax.sharding import PartitionSpec as P

learn_rate = 0.1
MESH = pl.DeviceIdType.MESH
BF = jnp.bfloat16
F32 = jnp.float32

D = 256
EDGES = 2048
NEG = 1024
PICKS = EDGES + NEG
UR = 128
IR = 256
PLANE = 4 * IR
BLK = 512


def one_hot_cols(index, width):
    lane = lax.broadcasted_iota(jnp.int32, index.shape, 1)
    parts = [
        jnp.where(index == lane + 128 * c, F32(1), F32(0)).astype(BF) for c in range(width // 128)
    ]
    return jnp.concatenate(parts, axis=1)


def one_hot_rows(index, base, rows):
    row = lax.broadcasted_iota(jnp.int32, (rows, index.shape[1]), 0) + base
    return jnp.where(row == index, F32(1), F32(0)).astype(BF)


def to_column(row):
    return jnp.broadcast_to(row, (128, 128)).T


def adagrad(table, state_ref, total, out_ref, out_state_ref):
    rows = total.shape[0]
    mean = jnp.sum(total * total, axis=1, keepdims=True) * (1.0 / D)
    for b in range(rows // 128):
        part = slice(128 * b, 128 * (b + 1))
        new_state = to_column(state_ref[:, part]) + mean[part]
        out_state_ref[:, part] = new_state.T[0:1, :]
        scale = learn_rate / jnp.sqrt(new_state)
        out_ref[part, :] = table[part, :] - total[part] * jnp.concatenate([scale, scale], axis=1)


def kernel(
    user_table_h, user_state_h, item_table_h, item_state_h, edge_users_h, edge_items_h, negatives_h,
    new_user_table, new_user_state, new_item_table, new_item_state,
    user_table, user_state, item_table, item_state, edge_users, edge_items, negatives, load_sem,
    items, users, turn, user_col, item_col, item_row, picked, picked_users, picked_negs, weights,
    user_grad, item_grad,
    user_keep, uxs, uxr, uys, uyr, keep, sib_s, sib_r, zs, zr,
    send_sem, recv_sem,
):
    u, t = lax.axis_index("user"), lax.axis_index("item")
    k, yl, z = lax.rem(u, 2), lax.rem(lax.div(u, 2), 2), lax.div(u, 4)
    yh, x = lax.rem(t, 2), lax.div(t, 2)
    ko, yo, ho = 1 - k, 1 - yl, 1 - yh
    zp, zm, z2 = lax.rem(z + 1, 4), lax.rem(z + 3, 4), lax.rem(z + 2, 4)
    xp, xm, x2 = lax.rem(x + 1, 4), lax.rem(x + 3, 4), lax.rem(x + 2, 4)

    def user_at(zz, yy, kk):
        return (zz * 2 + yy) * 2 + kk

    def user_peer(zz, yy, kk):
        return {"user": user_at(zz, yy, kk)}

    def item_peer(xx, yy):
        return {"item": xx * 2 + yy}

    sib, yn = user_peer(z, yl, ko), user_peer(z, yo, k)
    zup, zdn, zfar = user_peer(zp, yl, k), user_peer(zm, yl, k), user_peer(z2, yl, k)
    zup_o, zdn_o, zfar_o = user_peer(zp, yo, k), user_peer(zm, yo, k), user_peer(z2, yo, k)
    hn = item_peer(x, ho)
    xup, xdn, xfar = item_peer(xp, yh), item_peer(xm, yh), item_peer(x2, yh)
    peers = (sib, yn, zup, zdn, zfar, zup_o, zdn_o, zfar_o, hn, xup, xdn, xfar)

    barrier = pltpu.get_barrier_semaphore()
    for peer in peers:
        pl.semaphore_signal(barrier, inc=1, device_id=peer, device_id_type=MESH)

    pairs = (
        (item_table_h, item_table), (user_table_h, user_table), (edge_users_h, edge_users),
        (edge_items_h, edge_items), (negatives_h, negatives),
        (user_state_h, user_state), (item_state_h, item_state),
    )
    loads = [
        pltpu.make_async_copy(src, dst, load_sem.at[n]) for n, (src, dst) in enumerate(pairs)
    ]
    for load in loads:
        load.start()

    step = pl.when(u >= 0)

    copies = []

    def send(src, dst, peer):
        n = len(copies)
        copy = pltpu.make_async_remote_copy(
            src_ref=src, dst_ref=dst, send_sem=send_sem.at[n], recv_sem=recv_sem.at[n],
            device_id=peer, device_id_type=MESH,
        )
        copies.append(copy)
        copy.start()
        return copy

    def share(ref, peer):
        return send(ref, ref, peer)

    loads[0].wait()
    items[u] = item_table[...].astype(BF)
    loads[1].wait()
    users[t] = user_table[...].astype(BF)
    pl.semaphore_wait(barrier, len(peers))

    own_i, own_u = items.at[u], users.at[t]
    m_sib = share(own_i, sib)
    m_yn = share(own_i, yn)
    m_far = share(own_i, zfar)
    m_up = share(own_i, zup)
    m_dn = share(own_i, zdn)
    m_hn = share(own_u, hn)
    m_xup = share(own_u, xup)
    m_xdn = share(own_u, xdn)
    m_xfar = share(own_u, xfar)

    for load in loads[2:]:
        load.wait()
    @step
    def _():
        turn[...] = jnp.zeros_like(turn)
        item_tiles, neg_tiles = EDGES // 128, NEG // 128
        for b in range(item_tiles):
            part = slice(128 * b, 128 * (b + 1))
            turn[b:b + 1, :] = edge_items[0, :, part]
            turn[item_tiles + neg_tiles + b:item_tiles + neg_tiles + b + 1, :] = edge_users[0, :, part]
        for b in range(neg_tiles):
            turn[item_tiles + b:item_tiles + b + 1, :] = negatives[:, 128 * b:128 * (b + 1)]
        turned = turn[...].T
        for b in range(item_tiles + neg_tiles):
            item_col[128 * b:128 * (b + 1), :] = jnp.broadcast_to(turned[:, b:b + 1], (128, 128))
        for b in range(item_tiles):
            c = item_tiles + neg_tiles + b
            user_col[128 * b:128 * (b + 1), :] = jnp.broadcast_to(turned[:, c:c + 1], (128, 128))
        item_row[:, :EDGES] = edge_items[0, :, :]
        item_row[:, EDGES:] = negatives[...]

    def pick_half(zz, yy, first=False):
        @step
        def _():
            place = zz * 2 + yy
            half = items[pl.ds(place * 2, 2)].reshape(2 * IR, D)
            for b in range(PICKS // BLK):
                rows = pl.ds(b * BLK, BLK)
                one_hot = one_hot_cols(item_col[rows, :] - place * (2 * IR), 2 * IR)
                got = jnp.dot(one_hot, half, preferred_element_type=F32)
                picked[rows, :] = got if first else picked[rows, :] + got

    def item_shard(zz, yy):
        return items.at[user_at(zz, yy, k)]

    m_sib.wait_recv()
    pick_half(z, yl, True)

    m_yn.wait_recv()
    m_yup = share(item_shard(z, yo), zup)
    m_ydn = share(item_shard(z, yo), zdn)
    f_yn = share(item_shard(z, yo), sib)
    m_hn.wait_recv()
    near = users.at[x * 2 + ho]
    m_hup = share(near, xup)
    m_hdn = share(near, xdn)
    m_hfar = share(near, xfar)
    m_far.wait_recv()
    m_fary = share(item_shard(z2, yl), yn)
    f_far = share(item_shard(z2, yl), sib)
    m_up.wait_recv()
    f_dn = share(item_shard(zm, yl), sib)
    m_dn.wait_recv()
    f_up = share(item_shard(zp, yl), sib)

    f_yn.wait_recv()
    pick_half(z, yo)
    f_far.wait_recv()
    pick_half(z2, yl)
    f_dn.wait_recv()
    pick_half(zm, yl)
    m_yup.wait_recv()
    f_ydn = share(item_shard(zm, yo), sib)
    m_ydn.wait_recv()
    f_yup = share(item_shard(zp, yo), sib)
    f_up.wait_recv()
    pick_half(zp, yl)

    for copy in (m_xup, m_xdn, m_xfar, m_hup, m_hdn, m_hfar):
        copy.wait_recv()
    @step
    def _():
        for b in range(EDGES // BLK):
            rows = pl.ds(b * BLK, BLK)
            one_hot = one_hot_cols(user_col[rows, :], 8 * UR)
            got = jnp.dot(one_hot, users[...].reshape(8 * UR, D), preferred_element_type=F32)
            picked_users[rows, :] = got.astype(BF)

    m_fary.wait_recv()
    f_fary = share(item_shard(z2, yo), sib)
    f_ydn.wait_recv()
    pick_half(zm, yo)
    f_yup.wait_recv()
    pick_half(zp, yo)
    f_fary.wait_recv()
    pick_half(z2, yo)

    @step
    def _():
        picked_negs[...] = picked[EDGES:, :].astype(BF)
        for b in range(EDGES // BLK):
            rows = pl.ds(b * BLK, BLK)
            mine = picked_users[rows, :]
            wide = mine.astype(F32)
            item = picked[rows, :]
            scores = lax.dot_general(
                mine, picked_negs[...], (((1,), (1,)), ((), ())), preferred_element_type=F32
            )
            weights[rows, :] = (jax.nn.sigmoid(scores) * (1.0 / NEG)).astype(BF)
            positive = jnp.sum(wide * item, axis=1, keepdims=True)
            pull = jax.nn.sigmoid(-positive)
            picked[rows, :] = -pull * item
            item_grad[rows, :] = (-pull * wide).astype(BF)
        item_grad[EDGES:, :] = lax.dot_general(
            weights[...], picked_users[...], (((0,), (0,)), ((), ())), preferred_element_type=F32
        ).astype(BF)

    def spread_items(zz, yy, kk):
        one_hot = one_hot_rows(item_row[...], user_at(zz, yy, kk) * IR, IR)
        return jnp.dot(one_hot, item_grad[...], preferred_element_type=F32)

    def for_sib(n, places):
        @step
        def _():
            for m, (zz, yy) in enumerate(places):
                sib_s[n, m] = spread_items(zz, yy, ko).astype(BF)

        return send(sib_s.at[n], sib_r.at[n], sib)

    def for_core(n, places):
        @step
        def _():
            for m, (zz, yy) in enumerate(places):
                keep[n, m] = spread_items(zz, yy, k)

    def to_owners(n, copy, peers):
        copy.wait_recv()

        @step
        def _():
            for m in range(len(peers)):
                zs[n, m] = (keep[n, m] + sib_r[n, m].astype(F32)).astype(BF)

        return [send(zs.at[n, m], zr.at[n, m], peer) for m, peer in enumerate(peers)]

    far_two = ((z2, yl), (z2, yo))
    c0 = for_sib(0, far_two)
    for_core(0, far_two)
    o0 = to_owners(0, c0, (zfar, zfar_o))

    @step
    def _():
        for b in range(EDGES // BLK):
            rows = pl.ds(b * BLK, BLK)
            user_grad[rows, :] = (
                picked[rows, :]
                + jnp.dot(weights[rows, :], picked_negs[...], preferred_element_type=F32)
            ).astype(BF)

    def spread_users(xx):
        one_hot = one_hot_rows(edge_users[0, :, :], xx * (2 * UR), 2 * UR)
        got = jnp.dot(one_hot, user_grad[...], preferred_element_type=F32)
        return got.reshape(2, UR, D)

    x_copies = []
    for n, (xx, peer) in enumerate(((x2, xfar), (xp, xup), (xm, xdn))):
        @step
        def _():
            uxs[n] = spread_users(xx).astype(BF)

        x_copies.append(send(uxs.at[n], uxr.at[n], peer))

    @step
    def _():
        user_keep[...] = spread_users(x)


    other_two = ((zp, yo), (zm, yo))
    c1 = for_sib(1, other_two)
    for_core(1, other_two)
    o1 = to_owners(1, c1, (zup_o, zdn_o))
    same_two = ((zp, yl), (zm, yl))
    c2 = for_sib(2, same_two)
    for_core(2, same_two)
    own_two = ((z, yo), (z, yl))
    c3 = for_sib(3, own_two)
    o2 = to_owners(2, c2, (zup, zdn))
    for_core(3, own_two)
    o3 = to_owners(3, c3, (yn,))

    for copy in x_copies:
        copy.wait_recv()
    @step
    def _():
        uys[...] = (
            user_keep[ho] + uxr[0, ho].astype(F32) + uxr[1, ho].astype(F32) + uxr[2, ho].astype(F32)
        ).astype(BF)

    m_uy = send(uys, uyr, hn)

    m_uy.wait_recv()
    user_total = (
        user_keep[yh] + uxr[0, yh].astype(F32) + uxr[1, yh].astype(F32) + uxr[2, yh].astype(F32)
        + uyr[...].astype(F32)
    )
    adagrad(user_table, user_state, user_total, new_user_table, new_user_state)

    item_total = keep[3, 1] + sib_r[3, 1].astype(F32)
    for n, sent in enumerate((o0, o1, o2, o3)):
        for m, copy in enumerate(sent):
            copy.wait_recv()
            item_total = item_total + zr[n, m].astype(F32)
    adagrad(item_table, item_state, item_total, new_item_table, new_item_state)
    for copy in copies:
        copy.wait_send()


MESSAGES = 40


def store(*refs):
    sources, targets, sem = refs[:4], refs[4:8], refs[8]
    moves = [
        pltpu.make_async_copy(a, b, sem.at[n]) for n, (a, b) in enumerate(zip(sources, targets))
    ]
    for move in moves:
        move.start()
    for move in moves:
        move.wait()


def per_device(user_table, user_state, item_table, item_state, edge_users, edge_items, negatives):
    vmem = pl.BlockSpec(memory_space=pltpu.VMEM)
    hbm = pl.BlockSpec(memory_space=pltpu.HBM)
    local = [
        ((UR, D), F32), ((1, UR), F32), ((IR, D), F32), ((1, IR), F32),
        ((1, 1, EDGES), jnp.int32), ((1, 1, EDGES), jnp.int32), ((1, NEG), jnp.int32),
    ]
    scratch = [
        ((16, IR, D), BF),
        ((8, UR, D), BF),
        ((128, 128), jnp.int32),
        ((EDGES, 128), jnp.int32),
        ((PICKS, 128), jnp.int32),
        ((1, PICKS), jnp.int32),
        ((PICKS, D), F32),
        ((EDGES, D), BF),
        ((NEG, D), BF),
        ((EDGES, NEG), BF),
        ((EDGES, D), BF),
        ((PICKS, D), BF),
        ((2, UR, D), F32),
        ((3, 2, UR, D), BF),
        ((3, 2, UR, D), BF),
        ((UR, D), BF),
        ((UR, D), BF),
        ((4, 2, IR, D), F32),
        ((4, 2, IR, D), BF),
        ((4, 2, IR, D), BF),
        ((4, 2, IR, D), BF),
        ((4, 2, IR, D), BF),
    ]
    shapes = [jax.ShapeDtypeStruct(shape, kind) for shape, kind in local[:4]]
    out = pl.pallas_call(
        kernel,
        out_shape=[pltpu.VMEM(shape, kind) for shape, kind in local[:4]],
        in_specs=[hbm] * 7,
        out_specs=[vmem] * 4,
        scratch_shapes=[pltpu.VMEM(shape, kind) for shape, kind in local]
        + [pltpu.SemaphoreType.DMA((7,))]
        + [pltpu.VMEM(shape, kind) for shape, kind in scratch]
        + [pltpu.SemaphoreType.DMA((MESSAGES,)), pltpu.SemaphoreType.DMA((MESSAGES,))],
        compiler_params=pltpu.CompilerParams(
            collective_id=0, has_side_effects=True, vmem_limit_bytes=48 * 1024 * 1024
        ),
        name="step",
    )(
        *(
            pltpu.with_memory_space_constraint(a, pltpu.HBM)
            for a in (
                user_table, user_state.reshape(1, UR), item_table, item_state.reshape(1, IR),
                edge_users, edge_items, negatives,
            )
        )
    )
    out = pl.pallas_call(
        store,
        out_shape=shapes,
        in_specs=[vmem] * 4,
        out_specs=[hbm] * 4,
        scratch_shapes=[pltpu.SemaphoreType.DMA((4,))],
        compiler_params=pltpu.CompilerParams(vmem_limit_bytes=16 * 1024 * 1024),
        name="store",
    )(*(pltpu.with_memory_space_constraint(a, pltpu.VMEM) for a in out))
    return (out[0], out[1].reshape(UR), out[2], out[3].reshape(IR))


def solution(mesh):
    in_specs = (
        P(("user", "item"), None),
        P(("user", "item")),
        P(("item", "user"), None),
        P(("item", "user")),
        P("user", "item", None),
        P("user", "item", None),
        P("item", None),
    )
    out_specs = (
        P(("user", "item"), None),
        P(("user", "item")),
        P(("item", "user"), None),
        P(("item", "user")),
    )
    return jax.shard_map(
        per_device, mesh=mesh, in_specs=in_specs, out_specs=out_specs, check_vma=False
    )
```

time: 227 us -> 50 us (0.22)
  waiting for transfers between devices: 131 us -> 0 us
  Pallas kernels: 0 us -> 49.1 us
  matrix products: 40.6 us -> 0 us
  blocking collectives: 30.4 us -> 0 us
  between operations: 13.9 us -> 0.8 us
  other arithmetic: 9.11 us -> 0 us
    reduce_scatter x2 -> x0, waiting for transfers between devices: 125 us -> none  [the longest x1 68.1 us: per_device(): lax.psum_scatter(spread_rows(item_index, item_grad, item_owned * lax.axis...]
    pallas_call x0 -> x2, Pallas kernels: none -> 49.1 us  [the longest x1 48.3 us: per_device(): pl.pallas_call(kernel, out_shape=[pltpu.VMEM(shape, kind) for shape, kind...]
    dot_general x8 -> x0, matrix products: 40.6 us -> none  [the longest x3 17.3 us: spread_rows(): return jnp.dot(one_hot, values, preferred_element_type=jnp.float32)]
    all_gather x1 -> x0, blocking collectives: 30.4 us -> none  [per_device(): lax.all_gather(user_table.astype(jnp.bfloat16), 'item', axis=0, tiled=True)]
    all_gather x1 -> x0, waiting for transfers between devices: 5.99 us -> none  [per_device(): lax.all_gather(item_table.astype(jnp.bfloat16), 'user', axis=0, tiled=True)]
    sub x2 -> x0, other arithmetic: 3.41 us -> none  [adagrad(): table - learn_rate * gradient / jnp.sqrt(new_state)[:, None]]
    convert_element_type x2 -> x0, other arithmetic: 2.54 us -> none  [the longest x1 1.62 us: per_device(): item_table.astype(jnp.bfloat16)]
  transfers between devices with their start and end apart: 3 -> 0, of which waited for: 3 -> 0; matrix products, arithmetic and copies ran while one was open for 10% -> 0% of each run, Pallas kernels for 0% -> 0%
where the time goes in v3:
time: 50 us; the launch traced here: 49.9 us
  Pallas kernels  49.1 us (98%)
  between operations  0.8 us (2%)
    pallas_call x1, Pallas kernels, per_device(): pl.pallas_call(kernel, out_shape=[pltpu.VMEM(shape, kind) for shape, kind...  48.3 us

profile of v3, /device:TPU:1, one launch (start us, length us, event | category | flops | bytes accessed | tf_op | source)
XLA Modules:
  0.0 49.9 jit_solution(13018052340283429161)
XLA Ops:
  0.6 48.3 %step.1 = (f32[128,256]{1,0:T(8,128)S(1)}, f32[1,128]{1,0:T(1,128)S(1)}, f32[256,256]{1,0:T(8,128)S(1)}, f32[1,256]{1,0:T(1,128)S(1)}) custom-call(f32[128,256]{1,0:T(8,128)} %user_table_h.1, f32[1,128]{1,0:T(1,128)} %bitcast.5, f32[256,256]{1,0:T(8,128)} %item_table_h.1, f32[1,256]{1,0:T(1,128)} %bitcast.4, s32[1,1,2048]{2,1,0:T(1,128)} %edge_users_h.1, ...), custom_call_target="tpu_custom_call" | custom-call | tf_op jit(solution)/shard_map/step/pallas_call | solution.py:385
  48.9 0.8 %store.1 = (f32[128,256]{1,0:T(8,128)}, f32[1,128]{1,0:T(1,128)}, f32[256,256]{1,0:T(8,128)}, f32[1,256]{1,0:T(1,128)}) custom-call(f32[128,256]{1,0:T(8,128)S(1)} %get-tuple-element.12.refs_0_, f32[1,128]{1,0:T(1,128)S(1)} %get-tuple-element.13.refs_1_, f32[256,256]{1,0:T(8,128)S(1)} %get-tuple-element.14.refs_2_, f32[1,256]{1,0:T(1,128)S(1)} %get-tuple-element.15.refs_3_), custom_call_target="tpu_custom_call" | custom-call | tf_op jit(solution)/shard_map/store/pallas_call | solution.py:407

commit v4 on v3

--- a/solution.py
+++ b/solution.py
@@ -75,10 +75,10 @@
 
     sib, yn = user_peer(z, yl, ko), user_peer(z, yo, k)
     zup, zdn, zfar = user_peer(zp, yl, k), user_peer(zm, yl, k), user_peer(z2, yl, k)
-    zup_o, zdn_o, zfar_o = user_peer(zp, yo, k), user_peer(zm, yo, k), user_peer(z2, yo, k)
+    zup_o, zdn_o = user_peer(zp, yo, k), user_peer(zm, yo, k)
     hn = item_peer(x, ho)
     xup, xdn, xfar = item_peer(xp, yh), item_peer(xm, yh), item_peer(x2, yh)
-    peers = (sib, yn, zup, zdn, zfar, zup_o, zdn_o, zfar_o, hn, xup, xdn, xfar)
+    peers = (sib, yn, zup, zdn, zfar, zup_o, zdn_o, hn, xup, xdn, xfar)
 
     barrier = pltpu.get_barrier_semaphore()
     for peer in peers:
@@ -246,7 +246,8 @@
             for m, (zz, yy) in enumerate(places):
                 sib_s[n, m] = spread_items(zz, yy, ko).astype(BF)
 
-        return send(sib_s.at[n], sib_r.at[n], sib)
+        several = pl.ds(0, len(places))
+        return send(sib_s.at[n, several], sib_r.at[n, several], sib)
 
     def for_core(n, places):
         @step
@@ -254,20 +255,23 @@
             for m, (zz, yy) in enumerate(places):
                 keep[n, m] = spread_items(zz, yy, k)
 
-    def to_owners(n, copy, peers):
+    def to_owners(n, copy, peers, joined=False):
         copy.wait_recv()
 
         @step
         def _():
             for m in range(len(peers)):
-                zs[n, m] = (keep[n, m] + sib_r[n, m].astype(F32)).astype(BF)
+                total = keep[n, m] + sib_r[n, m].astype(F32)
+                if joined:
+                    total = total + zr[0, m].astype(F32)
+                zs[n, m] = total.astype(BF)
 
         return [send(zs.at[n, m], zr.at[n, m], peer) for m, peer in enumerate(peers)]
 
-    far_two = ((z2, yl), (z2, yo))
-    c0 = for_sib(0, far_two)
-    for_core(0, far_two)
-    o0 = to_owners(0, c0, (zfar, zfar_o))
+    first = ((z2, yl), (z2, yo), (z, yo))
+    c0 = for_sib(0, first)
+    for_core(0, first)
+    o0 = to_owners(0, c0, (zup, zdn, yn))
 
     @step
     def _():
@@ -283,31 +287,32 @@
         got = jnp.dot(one_hot, user_grad[...], preferred_element_type=F32)
         return got.reshape(2, UR, D)
 
-    x_copies = []
+    x_copies, x_same = [], []
     for n, (xx, peer) in enumerate(((x2, xfar), (xp, xup), (xm, xdn))):
         @step
         def _():
             uxs[n] = spread_users(xx).astype(BF)
 
-        x_copies.append(send(uxs.at[n], uxr.at[n], peer))
+        x_copies.append(send(uxs.at[n, ho], uxr.at[n, ho], peer))
+        x_same.append((n, peer))
 
     @step
     def _():
         user_keep[...] = spread_users(x)
 
 
-    other_two = ((zp, yo), (zm, yo))
-    c1 = for_sib(1, other_two)
-    for_core(1, other_two)
-    o1 = to_owners(1, c1, (zup_o, zdn_o))
-    same_two = ((zp, yl), (zm, yl))
-    c2 = for_sib(2, same_two)
-    for_core(2, same_two)
-    own_two = ((z, yo), (z, yl))
-    c3 = for_sib(3, own_two)
-    o2 = to_owners(2, c2, (zup, zdn))
-    for_core(3, own_two)
-    o3 = to_owners(3, c3, (yn,))
+    x_same = [send(uxs.at[n, yh], uxr.at[n, yh], peer) for n, peer in x_same]
+    alone_two = ((zp, yo), (zm, yl))
+    c1 = for_sib(1, alone_two)
+    for_core(1, alone_two)
+    o1 = to_owners(1, c1, (zup_o, zdn))
+    joined_two = ((zp, yl), (zm, yo))
+    c2 = for_sib(2, joined_two)
+    for_core(2, joined_two)
+    o0[0].wait_recv()
+    o0[1].wait_recv()
+    o2 = to_owners(2, c2, (zup, zdn_o), True)
+    c3 = for_sib(3, ((z, yl),))
 
     for copy in x_copies:
         copy.wait_recv()
@@ -318,6 +323,9 @@
         ).astype(BF)
 
     m_uy = send(uys, uyr, hn)
+    for_core(3, ((z, yl),))
+    for copy in x_same:
+        copy.wait_recv()
 
     m_uy.wait_recv()
     user_total = (
@@ -326,11 +334,12 @@
     )
     adagrad(user_table, user_state, user_total, new_user_table, new_user_state)
 
-    item_total = keep[3, 1] + sib_r[3, 1].astype(F32)
-    for n, sent in enumerate((o0, o1, o2, o3)):
-        for m, copy in enumerate(sent):
-            copy.wait_recv()
-            item_total = item_total + zr[n, m].astype(F32)
+    c3.wait_recv()
+    item_total = keep[3, 0] + sib_r[3, 0].astype(F32)
+    arrivals = ((0, 2, o0[2]), (1, 0, o1[0]), (1, 1, o1[1]), (2, 0, o2[0]), (2, 1, o2[1]))
+    for n, m, copy in arrivals:
+        copy.wait_recv()
+        item_total = item_total + zr[n, m].astype(F32)
     adagrad(item_table, item_state, item_total, new_item_table, new_item_state)
     for copy in copies:
         copy.wait_send()
@@ -375,11 +384,11 @@
         ((3, 2, UR, D), BF),
         ((UR, D), BF),
         ((UR, D), BF),
-        ((4, 2, IR, D), F32),
-        ((4, 2, IR, D), BF),
-        ((4, 2, IR, D), BF),
-        ((4, 2, IR, D), BF),
-        ((4, 2, IR, D), BF),
+        ((4, 3, IR, D), F32),
+        ((4, 3, IR, D), BF),
+        ((4, 3, IR, D), BF),
+        ((4, 3, IR, D), BF),
+        ((4, 3, IR, D), BF),
     ]
     shapes = [jax.ShapeDtypeStruct(shape, kind) for shape, kind in local[:4]]
     out = pl.pallas_call(

time: 50 us -> 49.2 us (0.984)
  Pallas kernels: 49.1 us -> 48.3 us
    pallas_call x1, Pallas kernels: 48.3 us -> 47.5 us  [per_device(): pl.pallas_call(kernel, out_shape=[pltpu.VMEM(shape, kind) for shape, kind...]
where the time goes in v4:
time: 49.2 us; the launch traced here: 49.1 us
  Pallas kernels  48.3 us (98%)
  between operations  0.8 us (2%)
    pallas_call x1, Pallas kernels, per_device(): pl.pallas_call(kernel, out_shape=[pltpu.VMEM(shape, kind) for shape, kind...  47.5 us

profile of v4, /device:TPU:1, one launch (start us, length us, event | category | flops | bytes accessed | tf_op | source)
XLA Modules:
  0.0 49.1 jit_solution(1138422049324078100)
XLA Ops:
  0.6 47.5 %step.1 = (f32[128,256]{1,0:T(8,128)S(1)}, f32[1,128]{1,0:T(1,128)S(1)}, f32[256,256]{1,0:T(8,128)S(1)}, f32[1,256]{1,0:T(1,128)S(1)}) custom-call(f32[128,256]{1,0:T(8,128)} %user_table_h.1, f32[1,128]{1,0:T(1,128)} %bitcast.5, f32[256,256]{1,0:T(8,128)} %item_table_h.1, f32[1,256]{1,0:T(1,128)} %bitcast.4, s32[1,1,2048]{2,1,0:T(1,128)} %edge_users_h.1, ...), custom_call_target="tpu_custom_call" | custom-call | tf_op jit(solution)/shard_map/step/pallas_call | solution.py:394
  48.1 0.8 %store.1 = (f32[128,256]{1,0:T(8,128)}, f32[1,128]{1,0:T(1,128)}, f32[256,256]{1,0:T(8,128)}, f32[1,256]{1,0:T(1,128)}) custom-call(f32[128,256]{1,0:T(8,128)S(1)} %get-tuple-element.12.refs_0_, f32[1,128]{1,0:T(1,128)S(1)} %get-tuple-element.13.refs_1_, f32[256,256]{1,0:T(8,128)S(1)} %get-tuple-element.14.refs_2_, f32[1,256]{1,0:T(1,128)S(1)} %get-tuple-element.15.refs_3_), custom_call_target="tpu_custom_call" | custom-call | tf_op jit(solution)/shard_map/store/pallas_call | solution.py:416

commit v5 on v4

--- a/solution.py
+++ b/solution.py
@@ -268,10 +268,13 @@
 
         return [send(zs.at[n, m], zr.at[n, m], peer) for m, peer in enumerate(peers)]
 
-    first = ((z2, yl), (z2, yo), (z, yo))
-    c0 = for_sib(0, first)
-    for_core(0, first)
-    o0 = to_owners(0, c0, (zup, zdn, yn))
+    far_two, own_one = ((z2, yl), (z2, yo)), ((z, yo),)
+    c0 = for_sib(0, far_two)
+    for_core(0, far_two)
+    c4 = for_sib(4, own_one)
+    o0 = to_owners(0, c0, (zup, zdn))
+    for_core(4, own_one)
+    o4 = to_owners(4, c4, (yn,))
 
     @step
     def _():
@@ -336,7 +339,7 @@
 
     c3.wait_recv()
     item_total = keep[3, 0] + sib_r[3, 0].astype(F32)
-    arrivals = ((0, 2, o0[2]), (1, 0, o1[0]), (1, 1, o1[1]), (2, 0, o2[0]), (2, 1, o2[1]))
+    arrivals = ((4, 0, o4[0]), (1, 0, o1[0]), (1, 1, o1[1]), (2, 0, o2[0]), (2, 1, o2[1]))
     for n, m, copy in arrivals:
         copy.wait_recv()
         item_total = item_total + zr[n, m].astype(F32)
@@ -345,7 +348,7 @@
         copy.wait_send()
 
 
-MESSAGES = 40
+MESSAGES = 48
 
 
 def store(*refs):
@@ -384,11 +387,11 @@
         ((3, 2, UR, D), BF),
         ((UR, D), BF),
         ((UR, D), BF),
-        ((4, 3, IR, D), F32),
-        ((4, 3, IR, D), BF),
-        ((4, 3, IR, D), BF),
-        ((4, 3, IR, D), BF),
-        ((4, 3, IR, D), BF),
+        ((5, 2, IR, D), F32),
+        ((5, 2, IR, D), BF),
+        ((5, 2, IR, D), BF),
+        ((5, 2, IR, D), BF),
+        ((5, 2, IR, D), BF),
     ]
     shapes = [jax.ShapeDtypeStruct(shape, kind) for shape, kind in local[:4]]
     out = pl.pallas_call(

time: 49.2 us -> 49.2 us (level)
  no operation moved by 1% of the time
where the time goes in v5:
time: 49.2 us; the launch traced here: 49.1 us
  Pallas kernels  48.2 us (98%)
  between operations  0.8 us (2%)
    pallas_call x1, Pallas kernels, per_device(): pl.pallas_call(kernel, out_shape=[pltpu.VMEM(shape, kind) for shape, kind...  47.5 us

profile of v5, /device:TPU:1, one launch (start us, length us, event | category | flops | bytes accessed | tf_op | source)
XLA Modules:
  0.0 49.1 jit_solution(4699192540115640243)
XLA Ops:
  0.6 47.5 %step.1 = (f32[128,256]{1,0:T(8,128)S(1)}, f32[1,128]{1,0:T(1,128)S(1)}, f32[256,256]{1,0:T(8,128)S(1)}, f32[1,256]{1,0:T(1,128)S(1)}) custom-call(f32[128,256]{1,0:T(8,128)} %user_table_h.1, f32[1,128]{1,0:T(1,128)} %bitcast.5, f32[256,256]{1,0:T(8,128)} %item_table_h.1, f32[1,256]{1,0:T(1,128)} %bitcast.4, s32[1,1,2048]{2,1,0:T(1,128)} %edge_users_h.1, ...), custom_call_target="tpu_custom_call" | custom-call | tf_op jit(solution)/shard_map/step/pallas_call | solution.py:397
  48.1 0.8 %store.1 = (f32[128,256]{1,0:T(8,128)}, f32[1,128]{1,0:T(1,128)}, f32[256,256]{1,0:T(8,128)}, f32[1,256]{1,0:T(1,128)}) custom-call(f32[128,256]{1,0:T(8,128)S(1)} %get-tuple-element.12.refs_0_, f32[1,128]{1,0:T(1,128)S(1)} %get-tuple-element.13.refs_1_, f32[256,256]{1,0:T(8,128)S(1)} %get-tuple-element.14.refs_2_, f32[1,256]{1,0:T(1,128)S(1)} %get-tuple-element.15.refs_3_), custom_call_target="tpu_custom_call" | custom-call | tf_op jit(solution)/shard_map/store/pallas_call | solution.py:419
